TPU v7x, 256 devices: a whole 4x4x8 slice. The times are simulated.
256 devices in a mesh: srow: 16 (over x, y_hi, core), scol: 16 (over z, y_lo).
Axes of the slice: x: 4, y: 4 (y_hi: 2, y_lo: 2; y = y_hi * 2 + y_lo), z: 8, core: 2. Of those that a mesh axis runs over, the one named last changes fastest.
Arguments:
- patterns: float32 [64, 64, 128, 128], P('srow', 'scol'), may hold values from 0.01 to 800, as said below
- offsets: int32 [64, 64, 2], P('srow', 'scol'), may hold values from 0 to 71, as said below
- object_field: float32 [2, 1152, 1152], P(None, 'srow', 'scol'), may hold values from -5 to 5
- probe: float32 [2, 2, 128, 128], replicated, may hold values from -6 to 6
Outputs:
- new_object: float32 [2, 1152, 1152], P(None, 'srow', 'scol')
- new_probe: float32 [2, 2, 128, 128], replicated
Inputs may be any that keep to these rules, and one draw needn't show every extreme that they name: `patterns`: patterns are positive. `offsets`: position (r, c) has its centre at tile row 16 * (r mod 4) plus 0 to 23, and tile column 16 * (c mod 4) plus 0 to 23.
All inputs are finite; a program needn't handle non-finite values.
Results may differ from a plain program's by a relative error of at most 0.0003.
Values sent between devices are 32-bit elements; how exact they have to be, the bound alone decides.
No kernel may reach another device: no remote copies, remote signals or barrier semaphores. Data moves between devices by JAX's collectives and lax.ppermute only.
A program may use at most 64 MiB of HBM per device.

v0:
```python
import math
import jax
import jax.numpy as jnp
from jax import lax
from jax.sharding import PartitionSpec as P

W = 128
PR = 4
PC = 4
obj_rate = 0.2
probe_rate = 0.5
amp_floor = 0.1
highest = lax.Precision.HIGHEST


def extended_2(cells, sides, width):
    for axis, dim in sides:
        count = lax.axis_size(axis)
        head = lax.slice_in_dim(cells, 0, width, axis=dim)
        tail = lax.slice_in_dim(cells, cells.shape[dim] - width, cells.shape[dim], axis=dim)
        cells = jnp.concatenate(
            [
                lax.ppermute(tail, axis, [(i, (i + 1) % count) for i in range(count)]),
                cells,
                lax.ppermute(head, axis, [((i + 1) % count, i) for i in range(count)]),
            ],
            axis=dim,
        )
    return cells


def signed_freq(length):
    counter = jnp.arange(length, dtype=jnp.int32)
    return ((counter + length // 2) % length - length // 2).astype(jnp.float32)


def dft_tables(length):
    counter = jnp.arange(length, dtype=jnp.int32)
    product = counter[:, None] * counter[None, :] % length
    angles = 2.0 * math.pi / length * product.astype(jnp.float32)
    return (jnp.cos(angles), jnp.sin(angles))


def rows_by(matrix, values):
    return jnp.einsum("uk,...kv->...uv", matrix, values, precision=highest)


def cols_by(values, matrix):
    return jnp.einsum("...uk,kv->...uv", values, matrix, precision=highest)


def transform(real_part, imag_part, cos_table, sin_table, turn_sign, real_only=False):
    length = cos_table.shape[0]
    if imag_part is None:
        first_re = rows_by(cos_table, real_part)
        first_im = turn_sign * rows_by(sin_table, real_part)
    else:
        first_re = rows_by(cos_table, real_part) - turn_sign * rows_by(sin_table, imag_part)
        first_im = rows_by(cos_table, imag_part) + turn_sign * rows_by(sin_table, real_part)
    second_re = (cols_by(first_re, cos_table) - turn_sign * cols_by(first_im, sin_table)) / length
    if real_only:
        return second_re
    second_im = (cols_by(first_im, cos_table) + turn_sign * cols_by(first_re, sin_table)) / length
    return (second_re, second_im)


def fold_rims(values, axis_dim, tile_len, half_width):
    full_len = values.shape[axis_dim]
    interior = lax.slice_in_dim(values, 2 * half_width, 2 * half_width + tile_len, axis=axis_dim)
    low_rim = lax.slice_in_dim(values, 0, half_width, axis=axis_dim)
    high_rim = lax.slice_in_dim(values, full_len - half_width, full_len, axis=axis_dim)
    low_pad = [
        (0, tile_len - half_width) if place == axis_dim else (0, 0) for place in range(values.ndim)
    ]
    high_pad = [
        (tile_len - half_width, 0) if place == axis_dim else (0, 0) for place in range(values.ndim)
    ]
    return interior + jnp.pad(low_rim, low_pad) + jnp.pad(high_rim, high_pad)


def on_device(patterns, offsets, object_field, probe):
    row_dev = lax.axis_size("srow")
    col_dev = lax.axis_size("scol")
    half_width = W // 2
    cos_table, sin_table = dft_tables(W)
    frequency = signed_freq(W)
    weights = jnp.sum(patterns, axis=(2, 3))
    com_row = jnp.einsum("abij,i->ab", patterns, frequency, precision=highest) / weights
    com_col = jnp.einsum("abij,j->ab", patterns, frequency, precision=highest) / weights
    centres = jnp.stack([com_row, com_col])
    row_pos = (
        (lax.axis_index("srow") * PR + jnp.arange(PR, dtype=jnp.int32)).astype(jnp.float32) + 0.5
    ) / (PR * row_dev) - 0.5
    col_pos = (
        (lax.axis_index("scol") * PC + jnp.arange(PC, dtype=jnp.int32)).astype(jnp.float32) + 0.5
    ) / (PC * col_dev) - 0.5
    row_grid = jnp.broadcast_to(row_pos[:, None], (PR, PC))
    col_grid = jnp.broadcast_to(col_pos[None, :], (PR, PC))
    first_sums = jnp.stack(
        [jnp.sum(weights), jnp.sum(weights * row_grid), jnp.sum(weights * col_grid)]
    )
    centre_moment = jnp.einsum("kab,ab->k", centres, weights, precision=highest)
    first_sums, centre_moment = lax.psum((first_sums, centre_moment), ("srow", "scol"))
    mean_row = first_sums[1] / first_sums[0]
    mean_col = first_sums[2] / first_sums[0]
    mean_centre = centre_moment / first_sums[0]
    spread = jnp.stack([row_grid - mean_row, col_grid - mean_col])
    deviation = centres - mean_centre[:, None, None]
    second_mom = jnp.einsum("iab,jab,ab->ij", spread, spread, weights, precision=highest)
    cross_mom = jnp.einsum("iab,kab,ab->ik", spread, deviation, weights, precision=highest)
    second_mom, cross_mom = lax.psum((second_mom, cross_mom), ("srow", "scol"))
    determ = second_mom[0, 0] * second_mom[1, 1] - second_mom[0, 1] * second_mom[1, 0]
    inverse = (
        jnp.stack(
            [
                jnp.stack([second_mom[1, 1], -second_mom[0, 1]]),
                jnp.stack([-second_mom[1, 0], second_mom[0, 0]]),
            ]
        )
        / determ
    )
    slopes = jnp.dot(inverse, cross_mom, precision=highest)
    descan = mean_centre[:, None, None] + jnp.einsum(
        "iab,ik->kab", spread, slopes, precision=highest
    )
    extended = extended_2(object_field, (("srow", 1), ("scol", 2)), half_width)
    pattern_flat = patterns.reshape(-1, W, W)
    spec_re, spec_im = transform(pattern_flat, None, cos_table, sin_table, -1.0)
    shift_r = descan[0].reshape(-1)
    shift_c = descan[1].reshape(-1)
    phases = (
        2.0
        * math.pi
        / W
        * (
            shift_r[:, None, None] * frequency[None, :, None]
            + shift_c[:, None, None] * frequency[None, None, :]
        )
    )
    turn_cos = jnp.cos(phases)
    turn_sin = jnp.sin(phases)
    rot_re = spec_re * turn_cos - spec_im * turn_sin
    rot_im = spec_re * turn_sin + spec_im * turn_cos
    shifted = transform(rot_re, rot_im, cos_table, sin_table, 1.0, real_only=True)
    targets = jnp.sqrt(jnp.maximum(shifted, 0.0))
    row_start = offsets[:, :, 0].reshape(-1)
    col_start = offsets[:, :, 1].reshape(-1)
    position_count = row_start.shape[0]

    def cut_one(place, gathered):
        corner = (jnp.int32(0), row_start[place], col_start[place])
        piece = lax.dynamic_slice(extended, corner, (2, W, W))
        return lax.dynamic_update_slice(
            gathered, piece[None], (place, jnp.int32(0), jnp.int32(0), jnp.int32(0))
        )

    windows = lax.fori_loop(
        0, position_count, cut_one, jnp.zeros((position_count, 2, W, W), jnp.float32)
    )
    win_re = windows[:, 0][:, None]
    win_im = windows[:, 1][:, None]
    probe_re = probe[:, 0][None]
    probe_im = probe[:, 1][None]
    exit_re = probe_re * win_re - probe_im * win_im
    exit_im = probe_re * win_im + probe_im * win_re
    far_re, far_im = transform(exit_re, exit_im, cos_table, sin_table, -1.0)
    amplitude = jnp.sqrt(jnp.sum(far_re * far_re + far_im * far_im, axis=1))
    factor = (1.0 - targets / jnp.maximum(amplitude, amp_floor))[:, None]
    back_re, back_im = transform(far_re * factor, far_im * factor, cos_table, sin_table, 1.0)
    grad_re = jnp.sum(probe_re * back_re + probe_im * back_im, axis=1)
    grad_im = jnp.sum(probe_re * back_im - probe_im * back_re, axis=1)
    probe_grad = jnp.stack(
        [
            jnp.sum(win_re * back_re + win_im * back_im, axis=0),
            jnp.sum(win_re * back_im - win_im * back_re, axis=0),
        ],
        axis=1,
    )
    grad_stack = jnp.stack([grad_re, grad_im], axis=1)

    def add_one(place, accum):
        corner = (jnp.int32(0), row_start[place], col_start[place])
        current = lax.dynamic_slice(accum, corner, (2, W, W))
        return lax.dynamic_update_slice(accum, current + grad_stack[place], corner)

    ext_grad = lax.fori_loop(0, position_count, add_one, jnp.zeros(extended.shape, jnp.float32))
    tile_rows = object_field.shape[1]
    tile_cols = object_field.shape[2]
    padded = extended_2(ext_grad, (("srow", 1), ("scol", 2)), half_width)
    grad_tile = fold_rims(fold_rims(padded, 1, tile_rows, half_width), 2, tile_cols, half_width)
    probe_power = jnp.max(jnp.sum(probe * probe, axis=(0, 1)))
    new_object = object_field - obj_rate * grad_tile / probe_power
    positions_all = PR * row_dev * PC * col_dev
    summed = lax.psum(probe_grad, ("srow", "scol"))
    new_probe = probe - probe_rate * summed / positions_all
    return (new_object, new_probe)


def solution(mesh):
    placed = (P("srow", "scol", None, None), P("srow", "scol", None), P(None, "srow", "scol"), P())
    return jax.shard_map(
        on_device,
        mesh=mesh,
        in_specs=placed,
        out_specs=(P(None, "srow", "scol"), P()),
        check_vma=False,
    )
```

profile of v0, /device:TPU:2, one launch (start us, length us, event | category | flops | bytes accessed | tf_op | source)
XLA Modules:
  0.0 756.6 jit_solution(8100221730847094329)
XLA Ops:
  7.2 2.3 fusion.302
  14.2 81.5 %all-reduce.3 = (f32[3]{0:T(128)S(1)}, f32[2]{0:T(128)S(1)}) all-reduce(f32[3]{0:T(128)S(1)} %pad_maximum_fusion.10, f32[2]{0:T(128)S(1)} %convolution_bitcast_fusion.4), channel_id=1, replica_groups=mesh['srow'=16,'scol'=16] {'srow','scol'}, use_global_device_ids=true, to_apply=%region_9.10 | all-reduce | flops 5 | bytes 40 | tf_op jit(solution)/shard_map/psum | solution.py:103
  101.5 73.2 %all-reduce.2 = (f32[2,2]{1,0:T(2,128)S(1)}, f32[2,2]{1,0:T(2,128)S(1)}) all-reduce(f32[2,2]{1,0:T(2,128)S(1)} %convolution_bitcast_fusion.2, f32[2,2]{1,0:T(2,128)S(1)} %convolution_bitcast_fusion.3), channel_id=1, replica_groups=mesh['srow'=16,'scol'=16] {'srow','scol'}, use_global_device_ids=true, to_apply=%region_11.12 | all-reduce | flops 8 | bytes 64 | tf_op jit(solution)/shard_map/psum | solution.py:111
  188.7 6.0 fusion.95
  194.7 5.8 fusion.99
  200.5 7.0 fusion.45
  207.5 5.8 fusion.46
  213.4 2.9 fusion.97
  217.3 4.1 collective-permute-start.3
  221.8 4.5 collective-permute-done.2
  226.3 3.8 collective-permute-done.3
  231.2 80.8 %while.26 = (s32[]{:T(128)}, f32[16,2,128,128]{3,2,0,1:T(8,128)S(1)}, s32[16]{0:T(128)S(1)}, s32[16]{0:T(128)S(1)}, f32[2,200,200]{2,1,0:T(8,128)S(1)}, /*index=5*/s32[]{:T(128)}, s32[]{:T(128)}, s32[]{:T(128)}) while((s32[]{:T(128)}, f32[16,2,128,128]{3,2,0,1:T(8,128)S(1)}, s32[16]{0:T(128)S(1)}, s32[16]{0:T(128)S(1)}, ...), condition=%wide.region_1.2_spmd, body=%wide.region_0.1_spmd.sunk | while | flops 8 | bytes 262333 | solution.py:157
  322.3 3.6 fusion.10
  325.9 3.7 fusion.8
  331.8 3.6 multiply_subtract_fusion
  335.4 3.9 add_reduce_fusion.2
  339.3 2.4 fusion.56
  341.7 3.6 fusion.22
  345.3 3.6 fusion.20
  348.9 4.1 fusion.31
  353.0 3.7 fusion.2
  356.6 3.7 fusion
  360.5 3.8 fusion.28
  364.4 3.6 fusion.38
  368.0 5.0 add_reduce_fusion
  373.2 119.0 %while.27 = (s32[]{:T(128)}, f32[2,200,200]{2,1,0:T(8,128)S(1)}, s32[16]{0:T(128)S(1)}, s32[16]{0:T(128)S(1)}, f32[16,2,128,128]{3,2,1,0:T(8,128)S(1)}, /*index=5*/s32[]{:T(128)}, s32[]{:T(128)}, s32[]{:T(128)}) while((s32[]{:T(128)}, f32[2,200,200]{2,1,0:T(8,128)S(1)}, s32[16]{0:T(128)S(1)}, s32[16]{0:T(128)S(1)}, ...), condition=%wide.region_16.17_spmd, body=%wide.region_15.16_spmd.sunk | while | flops 32776 | bytes 655553 | solution.py:186
  378.4 2.3 dynamic_update_slice.18
  385.9 2.3 dynamic_update_slice.18
  401.0 2.3 dynamic_update_slice.18
  493.1 4.2 collective-permute-start.5
  500.1 4.1 collective-permute-start.7
  504.2 241.1 %all-reduce.6.cloned.1.call-done = f32[2,2,128,128]{3,2,1,0:T(8,128)} async-done(((f32[2,2,128,128]{3,2,1,0:T(8,128)}), f32[2,2,128,128]{3,2,1,0:T(8,128)}) %all-reduce.6.cloned.1.call-update) | async-done | bytes 262160 | tf_op jit(solution)/shard_map/psum | solution.py:194
  (211 shorter events, 111.9 us)
Async XLA Ops:
  7.2 170.6 %copy-start = (f32[4,4,128,128]{3,2,1,0:T(8,128)S(1)}, f32[4,4,128,128]{3,2,1,0:T(8,128)}, u32[]{:S(2)}) copy-start(f32[4,4,128,128]{3,2,1,0:T(8,128)} %param.8) | copy-start | bytes 3145732
  7.2 738.2 %all-reduce.6.cloned.1.call-start = ((), (), s32[]{:S(2)}) async-start(), calls=%async_computation | async-start | bytes 524288 | tf_op jit(solution)/shard_map/psum | solution.py:194
  14.1 202.9 %collective-permute-start = (f32[2,64,72]{2,1,0:T(8,128)S(1)}, f32[2,64,72]{2,1,0:T(8,128)S(1)}, u32[]{:S(2)}, u32[]{:S(2)}) collective-permute-start(f32[2,64,72]{2,1,0:T(8,128)S(1)} %get-tuple-element.249), channel_id=1, source_target_pairs={{0,16},{16,32},{32,48},{48,64},{64,80},{80,96},{96,112},{112,128},... | collective-permute-start | bytes 110600 | tf_op jit(solution)/shard_map/ppermute | solution.py:23
  100.3 116.8 %collective-permute-start.1 = (f32[2,64,72]{2,1,0:T(8,128)S(1)}, f32[2,64,72]{2,1,0:T(8,128)S(1)}, u32[]{:S(2)}, u32[]{:S(2)}) collective-permute-start(f32[2,64,72]{2,1,0:T(8,128)S(1)} %get-tuple-element.248), channel_id=1, source_target_pairs={{16,0},{32,16},{48,32},{64,48},{80,64},{96,80},{112,96},{128,112},... | collective-permute-start | bytes 110600 | tf_op jit(solution)/shard_map/ppermute | solution.py:25
  213.3 3.0 copy-start.3
  213.3 3.7 copy-start.5
  213.3 8.1 %copy-start.10 = (s32[4,4,2]{1,2,0:T(2,128)S(1)}, s32[4,4,2]{1,2,0:T(2,128)}, u32[]{:S(2)}) copy-start(s32[4,4,2]{1,2,0:T(2,128)} %param.9) | copy-start | bytes 388
  217.2 9.1 %collective-permute-start.2 = (f32[2,200,64]{2,1,0:T(8,128)S(1)}, f32[2,200,64]{2,1,0:T(8,128)S(1)}, u32[]{:S(2)}, u32[]{:S(2)}) collective-permute-start(f32[2,200,64]{2,1,0:T(8,128)S(1)} %get-tuple-element.246), channel_id=1, source_target_pairs={{0,1},{1,2},{2,3},{3,4},{4,5},{5,6},{6,7},{7,8},{8,9},{9,10},{10,1... | collective-permute-start | bytes 307208 | tf_op jit(solution)/shard_map/ppermute | solution.py:23
  217.3 12.8 %collective-permute-start.3 = (f32[2,200,64]{2,1,0:T(8,128)S(1)}, f32[2,200,64]{2,1,0:T(8,128)}, u32[]{:S(2)}, u32[]{:S(2)}) collective-permute-start(f32[2,200,64]{2,1,0:T(8,128)S(1)} %get-tuple-element.247), channel_id=1, source_target_pairs={{1,0},{2,1},{3,2},{4,3},{5,4},{6,5},{7,6},{8,7},{9,8},{10,9},{11,1... | collective-permute-start | bytes 307208 | tf_op jit(solution)/shard_map/ppermute | solution.py:25
  312.0 1.7 copy-start.1
  335.4 3.9 copy-start.6
  335.4 3.9 copy-start.7
  356.6 3.7 copy-start.2
  364.4 3.6 copy-start.8
  364.4 3.6 copy-start.9
  492.2 253.1 %copy-start.4 = (f32[2,2,128,128]{3,2,1,0:T(8,128)S(1)}, f32[2,2,128,128]{3,2,1,0:T(8,128)}, u32[]{:S(2)}) copy-start(f32[2,2,128,128]{3,2,1,0:T(8,128)} %param.11) | copy-start | bytes 786436
  492.3 6.9 collective-permute-start.4
  492.4 255.4 %copy-start.11 = (pred[72]{0:T(512)(128)(4,1)S(1)}, pred[72]{0:T(512)(128)(4,1)}, u32[]{:S(2)}) copy-start(pred[72]{0:T(512)(128)(4,1)} %constant.140.clone.1) | copy-start | bytes 220
  493.1 6.7 collective-permute-start.5
  500.0 247.8 %collective-permute-start.6 = (f32[2,328,64]{2,1,0:T(8,128)S(1)}, f32[2,328,64]{2,1,0:T(8,128)S(1)}, u32[]{:S(2)}, u32[]{:S(2)}) collective-permute-start(f32[2,328,64]{2,1,0:T(8,128)S(1)} %get-tuple-element.236), channel_id=1, source_target_pairs={{0,1},{1,2},{2,3},{3,4},{4,5},{5,6},{6,7},{7,8},{8,9},{9,10},{10,1... | collective-permute-start | bytes 503816 | tf_op jit(solution)/shard_map/ppermute | solution.py:23
  500.1 247.7 %collective-permute-start.7 = (f32[2,328,64]{2,1,0:T(8,128)S(1)}, f32[2,328,64]{2,1,0:T(8,128)S(1)}, u32[]{:S(2)}, u32[]{:S(2)}) collective-permute-start(f32[2,328,64]{2,1,0:T(8,128)S(1)} %get-tuple-element.237), channel_id=1, source_target_pairs={{1,0},{2,1},{3,2},{4,3},{5,4},{6,5},{7,6},{8,7},{9,8},{10,9},{11,1... | collective-permute-start | bytes 503816 | tf_op jit(solution)/shard_map/ppermute | solution.py:25
Sparse Core Ops, SparseCore 0:
  493.2 252.0 all-reduce.5
where the time goes:
time: 763 us; the launch traced here: 757 us
  waiting for transfers between devices  252 us (33%)
  blocking collectives  155 us (20%)
  loops' own time  122 us (16%)
  matrix products  93.4 us (12%)
  local copies, waits for them, and re-layouts  83.1 us (11%)
  between operations  21.2 us (3%)
  other arithmetic  16.3 us (2%)
  starting transfers between devices  14 us (2%)
    psum x1, waiting for transfers between devices, on_device(): summed = lax.psum(probe_grad, ('srow', 'scol'))  241 us
    psum x1, blocking collectives, on_device(): lax.psum((first_sums, centre_moment), ('srow', 'scol'))  81.5 us
    psum x1, blocking collectives, on_device(): second_mom, cross_mom = lax.psum((second_mom, cross_mom), ('srow', 'scol'))  73.2 us
    another operation x1, loops' own time, on_device(): lax.fori_loop(0, position_count, add_one, jnp.zeros(extended.shape, jnp.f...  62.7 us
    another operation x1, loops' own time, on_device(): lax.fori_loop(0, position_count, cut_one, jnp.zeros((position_count, 2, W...  59.2 us
    dot_general x14, matrix products, rows_by(): return jnp.einsum('uk,...kv->...uv', matrix, values, precision=highest)  51.1 us
    dot_general x14, matrix products, cols_by(): return jnp.einsum('...uk,kv->...uv', values, matrix, precision=highest)  40.9 us
    dynamic_update_slice x16, local copies, waits for them, and re-layouts, add_one(): return lax.dynamic_update_slice(accum, current + grad_stack[place], corner)  35.7 us
  transfers between devices with their start and end apart: 9, of which 5 were waited for; matrix products, arithmetic and copies ran while one was open for 6% of the time, Pallas kernels for 0%

commit v1 on v0

--- a/solution.py
+++ b/solution.py
@@ -191,7 +191,7 @@
     probe_power = jnp.max(jnp.sum(probe * probe, axis=(0, 1)))
     new_object = object_field - obj_rate * grad_tile / probe_power
     positions_all = PR * row_dev * PC * col_dev
-    summed = lax.psum(probe_grad, ("srow", "scol"))
+    summed = lax.psum(lax.psum(probe_grad, "srow"), "scol")
     new_probe = probe - probe_rate * summed / positions_all
     return (new_object, new_probe)
 

time: 763 us -> 793 us (1.039)
  waiting for transfers between devices: 252 us -> 282 us
    psum x1 -> x2, waiting for transfers between devices: 241 us -> 271 us  [on_device(): summed = lax.psum(lax.psum(probe_grad, 'srow'), 'scol')]
  transfers between devices with their start and end apart: 9 -> 10, of which waited for: 5 -> 6; matrix products, arithmetic and copies ran while one was open for 6% -> 5% of each run, Pallas kernels for 0% -> 0%
where the time goes in v1:
time: 793 us; the launch traced here: 787 us
  waiting for transfers between devices  282 us (36%)
  blocking collectives  155 us (20%)
  loops' own time  122 us (15%)
  matrix products  94 us (12%)
  local copies, waits for them, and re-layouts  82.9 us (10%)
  between operations  21.3 us (3%)
  other arithmetic  16.3 us (2%)
  starting transfers between devices  14 us (2%)
    psum x2, waiting for transfers between devices, on_device(): summed = lax.psum(lax.psum(probe_grad, 'srow'), 'scol')  271 us
    psum x1, blocking collectives, on_device(): lax.psum((first_sums, centre_moment), ('srow', 'scol'))  81.5 us
    psum x1, blocking collectives, on_device(): second_mom, cross_mom = lax.psum((second_mom, cross_mom), ('srow', 'scol'))  73.3 us
    another operation x1, loops' own time, on_device(): lax.fori_loop(0, position_count, add_one, jnp.zeros(extended.shape, jnp.f...  62.7 us
    another operation x1, loops' own time, on_device(): lax.fori_loop(0, position_count, cut_one, jnp.zeros((position_count, 2, W...  59.2 us
    dot_general x14, matrix products, rows_by(): return jnp.einsum('uk,...kv->...uv', matrix, values, precision=highest)  51.4 us
    dot_general x14, matrix products, cols_by(): return jnp.einsum('...uk,kv->...uv', values, matrix, precision=highest)  41.1 us
    dynamic_update_slice x16, local copies, waits for them, and re-layouts, add_one(): return lax.dynamic_update_slice(accum, current + grad_stack[place], corner)  35.5 us
  transfers between devices with their start and end apart: 10, of which 6 were waited for; matrix products, arithmetic and copies ran while one was open for 5% of the time, Pallas kernels for 0%

profile of v1, /device:TPU:2, one launch (start us, length us, event | category | flops | bytes accessed | tf_op | source)
XLA Modules:
  0.0 787.3 jit_solution(7100399150542651007)
XLA Ops:
  7.2 2.3 fusion.302
  14.2 81.5 %all-reduce.3 = (f32[3]{0:T(128)S(1)}, f32[2]{0:T(128)S(1)}) all-reduce(f32[3]{0:T(128)S(1)} %pad_maximum_fusion.10, f32[2]{0:T(128)S(1)} %convolution_bitcast_fusion.4), channel_id=1, replica_groups=mesh['srow'=16,'scol'=16] {'srow','scol'}, use_global_device_ids=true, to_apply=%region_9.10 | all-reduce | flops 5 | bytes 40 | tf_op jit(solution)/shard_map/psum | solution.py:103
  101.5 73.3 %all-reduce.2 = (f32[2,2]{1,0:T(2,128)S(1)}, f32[2,2]{1,0:T(2,128)S(1)}) all-reduce(f32[2,2]{1,0:T(2,128)S(1)} %convolution_bitcast_fusion.2, f32[2,2]{1,0:T(2,128)S(1)} %convolution_bitcast_fusion.3), channel_id=1, replica_groups=mesh['srow'=16,'scol'=16] {'srow','scol'}, use_global_device_ids=true, to_apply=%region_11.12 | all-reduce | flops 8 | bytes 64 | tf_op jit(solution)/shard_map/psum | solution.py:111
  188.6 6.0 fusion.95
  194.6 5.8 fusion.99
  200.4 7.0 fusion.45
  207.4 5.8 fusion.46
  213.2 2.9 fusion.97
  217.2 4.1 collective-permute-start.3
  221.7 4.5 collective-permute-done.2
  226.2 3.8 collective-permute-done.3
  231.1 80.8 %while.26 = (s32[]{:T(128)}, f32[16,2,128,128]{3,2,0,1:T(8,128)S(1)}, s32[16]{0:T(128)S(1)}, s32[16]{0:T(128)S(1)}, f32[2,200,200]{2,1,0:T(8,128)S(1)}, /*index=5*/s32[]{:T(128)}, s32[]{:T(128)}, s32[]{:T(128)}) while((s32[]{:T(128)}, f32[16,2,128,128]{3,2,0,1:T(8,128)S(1)}, s32[16]{0:T(128)S(1)}, s32[16]{0:T(128)S(1)}, ...), condition=%wide.region_1.2_spmd, body=%wide.region_0.1_spmd.sunk | while | flops 8 | bytes 262333 | solution.py:157
  322.3 3.6 fusion.10
  325.9 3.8 fusion.8
  331.9 3.6 multiply_subtract_fusion
  335.5 4.0 add_reduce_fusion.2
  339.6 2.4 fusion.56
  342.0 3.6 fusion.22
  345.6 3.6 fusion.20
  349.3 4.1 fusion.31
  353.4 3.7 fusion.2
  357.1 3.6 fusion
  360.9 3.9 fusion.28
  364.8 3.6 fusion.38
  368.5 5.1 add_reduce_fusion
  373.8 118.8 %while.27 = (s32[]{:T(128)}, f32[2,200,200]{2,1,0:T(8,128)S(1)}, s32[16]{0:T(128)S(1)}, s32[16]{0:T(128)S(1)}, f32[16,2,128,128]{3,2,1,0:T(8,128)S(1)}, /*index=5*/s32[]{:T(128)}, s32[]{:T(128)}, s32[]{:T(128)}) while((s32[]{:T(128)}, f32[2,200,200]{2,1,0:T(8,128)S(1)}, s32[16]{0:T(128)S(1)}, s32[16]{0:T(128)S(1)}, ...), condition=%wide.region_16.17_spmd, body=%wide.region_15.16_spmd.sunk | while | flops 32776 | bytes 655553 | solution.py:186
  386.5 2.3 dynamic_update_slice.18
  401.6 2.3 dynamic_update_slice.18
  493.6 4.2 collective-permute-start.5
  500.6 4.1 collective-permute-start.7
  504.7 125.4 %all-reduce.7.cloned.1.call-done = f32[2,2,128,128]{3,2,1,0:T(8,128)} async-done(((f32[2,2,128,128]{3,2,1,0:T(8,128)}), f32[2,2,128,128]{3,2,1,0:T(8,128)}) %all-reduce.7.cloned.1.call-update) | async-done | bytes 262160 | tf_op jit(solution)/shard_map/psum | solution.py:194
  630.5 145.9 %all-reduce.9.cloned.1.call-done = f32[2,2,128,128]{3,2,1,0:T(8,128)} async-done(((f32[2,2,128,128]{3,2,1,0:T(8,128)}), f32[2,2,128,128]{3,2,1,0:T(8,128)}) %all-reduce.9.cloned.1.call-update) | async-done | bytes 262160 | tf_op jit(solution)/shard_map/psum | solution.py:194
  (214 shorter events, 114.3 us)
Async XLA Ops:
  7.2 170.6 %copy-start = (f32[4,4,128,128]{3,2,1,0:T(8,128)S(1)}, f32[4,4,128,128]{3,2,1,0:T(8,128)}, u32[]{:S(2)}) copy-start(f32[4,4,128,128]{3,2,1,0:T(8,128)} %param.8) | copy-start | bytes 3145732
  7.2 622.9 %all-reduce.7.cloned.1.call-start = ((), (), s32[]{:S(2)}) async-start(), calls=%async_computation | async-start | bytes 524288 | tf_op jit(solution)/shard_map/psum | solution.py:194
  14.1 202.7 %collective-permute-start = (f32[2,64,72]{2,1,0:T(8,128)S(1)}, f32[2,64,72]{2,1,0:T(8,128)S(1)}, u32[]{:S(2)}, u32[]{:S(2)}) collective-permute-start(f32[2,64,72]{2,1,0:T(8,128)S(1)} %get-tuple-element.249), channel_id=1, source_target_pairs={{0,16},{16,32},{32,48},{48,64},{64,80},{80,96},{96,112},{112,128},... | collective-permute-start | bytes 110600 | tf_op jit(solution)/shard_map/ppermute | solution.py:23
  100.3 116.7 %collective-permute-start.1 = (f32[2,64,72]{2,1,0:T(8,128)S(1)}, f32[2,64,72]{2,1,0:T(8,128)S(1)}, u32[]{:S(2)}, u32[]{:S(2)}) collective-permute-start(f32[2,64,72]{2,1,0:T(8,128)S(1)} %get-tuple-element.248), channel_id=1, source_target_pairs={{16,0},{32,16},{48,32},{64,48},{80,64},{96,80},{112,96},{128,112},... | collective-permute-start | bytes 110600 | tf_op jit(solution)/shard_map/ppermute | solution.py:25
  213.2 3.0 copy-start.3
  213.2 3.7 copy-start.5
  213.2 8.1 %copy-start.10 = (s32[4,4,2]{1,2,0:T(2,128)S(1)}, s32[4,4,2]{1,2,0:T(2,128)}, u32[]{:S(2)}) copy-start(s32[4,4,2]{1,2,0:T(2,128)} %param.9) | copy-start | bytes 388
  217.1 9.1 %collective-permute-start.2 = (f32[2,200,64]{2,1,0:T(8,128)S(1)}, f32[2,200,64]{2,1,0:T(8,128)S(1)}, u32[]{:S(2)}, u32[]{:S(2)}) collective-permute-start(f32[2,200,64]{2,1,0:T(8,128)S(1)} %get-tuple-element.246), channel_id=1, source_target_pairs={{0,1},{1,2},{2,3},{3,4},{4,5},{5,6},{6,7},{7,8},{8,9},{9,10},{10,1... | collective-permute-start | bytes 307208 | tf_op jit(solution)/shard_map/ppermute | solution.py:23
  217.2 12.8 %collective-permute-start.3 = (f32[2,200,64]{2,1,0:T(8,128)S(1)}, f32[2,200,64]{2,1,0:T(8,128)}, u32[]{:S(2)}, u32[]{:S(2)}) collective-permute-start(f32[2,200,64]{2,1,0:T(8,128)S(1)} %get-tuple-element.247), channel_id=1, source_target_pairs={{1,0},{2,1},{3,2},{4,3},{5,4},{6,5},{7,6},{8,7},{9,8},{10,9},{11,1... | collective-permute-start | bytes 307208 | tf_op jit(solution)/shard_map/ppermute | solution.py:25
  311.9 1.7 copy-start.1
  335.5 4.0 copy-start.6
  335.5 4.0 copy-start.7
  357.1 3.6 copy-start.2
  364.8 3.6 copy-start.8
  364.8 3.6 copy-start.9
  492.7 137.5 %copy-start.11 = (pred[72]{0:T(512)(128)(4,1)S(1)}, pred[72]{0:T(512)(128)(4,1)}, u32[]{:S(2)}) copy-start(pred[72]{0:T(512)(128)(4,1)} %constant.140.clone.1) | copy-start | bytes 220
  492.7 6.9 collective-permute-start.4
  493.5 282.9 %all-reduce.9.cloned.1.call-start = ((), (), s32[]{:S(2)}) async-start(), calls=%async_computation.1 | async-start | bytes 524288 | tf_op jit(solution)/shard_map/psum | solution.py:194
  493.6 6.7 collective-permute-start.5
  499.6 276.8 %copy-start.4 = (f32[2,2,128,128]{3,2,1,0:T(8,128)S(1)}, f32[2,2,128,128]{3,2,1,0:T(8,128)}, u32[]{:S(2)}) copy-start(f32[2,2,128,128]{3,2,1,0:T(8,128)} %param.11) | copy-start | bytes 786436
  500.5 129.6 %collective-permute-start.6 = (f32[2,328,64]{2,1,0:T(8,128)S(1)}, f32[2,328,64]{2,1,0:T(8,128)S(1)}, u32[]{:S(2)}, u32[]{:S(2)}) collective-permute-start(f32[2,328,64]{2,1,0:T(8,128)S(1)} %get-tuple-element.236), channel_id=1, source_target_pairs={{0,1},{1,2},{2,3},{3,4},{4,5},{5,6},{6,7},{7,8},{8,9},{9,10},{10,1... | collective-permute-start | bytes 503816 | tf_op jit(solution)/shard_map/ppermute | solution.py:23
  500.6 129.6 %collective-permute-start.7 = (f32[2,328,64]{2,1,0:T(8,128)S(1)}, f32[2,328,64]{2,1,0:T(8,128)S(1)}, u32[]{:S(2)}, u32[]{:S(2)}) collective-permute-start(f32[2,328,64]{2,1,0:T(8,128)S(1)} %get-tuple-element.237), channel_id=1, source_target_pairs={{1,0},{2,1},{3,2},{4,3},{5,4},{6,5},{7,6},{8,7},{9,8},{10,9},{11,1... | collective-permute-start | bytes 503816 | tf_op jit(solution)/shard_map/ppermute | solution.py:25
Sparse Core Ops, SparseCore 0:
  493.6 136.3 all-reduce.6
  632.9 143.5 all-reduce.8
